TPU v7x, 32 devices: a whole 2x2x4 slice. The times are simulated.
32 devices in a mesh: gx: 8 (over z, y), gz: 4 (over x, core).
Axes of the slice: x: 2, y: 2, z: 4, core: 2. Of those that a mesh axis runs over, the one named last changes fastest.
Arguments:
- whitened: float32 [2, 64, 1024, 512], P(None, 'gz', 'gx'), may hold values from -6 to 6
- observed: float32 [2, 1024, 512], P(None, 'gx'), may hold values from -12 to 12
- lower_x: bfloat16 [1024, 1024], P('gx'), as said below
- lower_y: bfloat16 [512, 512], P('gx'), as said below
- lower_z: bfloat16 [64, 64], replicated, as said below
- coupling_kernel: float32 [2, 3, 3, 3], replicated, may hold values from -1.25 to 1.25
Outputs:
- gradient: float32 [2, 64, 1024, 512], P(None, 'gz', 'gx')
- misfit: float32 [2, 1024, 512], P(None, 'gx')
Inputs may be any that keep to these rules, and one draw needn't show every extreme that they name: `lower_x`: lower triangular: zero above the diagonal, diagonal entries between 0.5 and 1.5. `lower_y`: lower triangular: zero above the diagonal, diagonal entries between 0.5 and 1.5. `lower_z`: lower triangular: zero above the diagonal, diagonal entries between 0.5 and 1.5.
All inputs are finite; a program needn't handle non-finite values.
Results may differ from a plain program's by a relative error of at most 0.013.
The roundings to bfloat16 on the way count: a program that leaves them out, or rounds other values in their place, can miss the bound.
Values may be sent and summed in bfloat16 or wider, within the bound.
A program may use at most 128 MiB of HBM per device.

v0:
```python
import math
import jax
import jax.numpy as jnp
from jax import lax
from jax.sharding import PartitionSpec as P

NZ = 64


def padded_2(x, sides, width):
    for axis, dim in sides:
        peers, length = (lax.axis_size(axis), x.shape[dim])
        up = [(i, (i + 1) % peers) for i in range(peers - 1)]
        down = [(j, i) for i, j in up]
        last = lax.slice_in_dim(x, length - width, length, axis=dim)
        first = lax.slice_in_dim(x, 0, width, axis=dim)
        before = lax.ppermute(last, axis, up)
        after = lax.ppermute(first, axis, down)
        x = jnp.concatenate([before, x, after], axis=dim)
    return x


def depth_lines(values, local_step):
    turned = lax.all_to_all(values, "gz", split_axis=3, concat_axis=1, tiled=True)
    return lax.all_to_all(local_step(turned), "gz", split_axis=1, concat_axis=3, tiled=True)


def across_lines(values, local_step):
    turned = lax.all_to_all(values, "gx", split_axis=3, concat_axis=2, tiled=True)
    return lax.all_to_all(local_step(turned), "gx", split_axis=2, concat_axis=3, tiled=True)


def stencil_sum(padded, kernel, depth_rows, x_rows, y_rows, flipped):
    total = jnp.zeros(padded.shape[:-3] + (depth_rows, x_rows, y_rows), jnp.float32)
    for offset_z in range(3):
        for offset_x in range(3):
            for offset_y in range(3):
                start_z = 2 - offset_z if flipped else offset_z
                start_x = 2 - offset_x if flipped else offset_x
                start_y = 2 - offset_y if flipped else offset_y
                total = (
                    total
                    + kernel[offset_z, offset_x, offset_y]
                    * padded[
                        ...,
                        start_z : start_z + depth_rows,
                        start_x : start_x + x_rows,
                        start_y : start_y + y_rows,
                    ]
                )
    return total


def depth_weights(first_row, depth_rows):
    depth = (first_row + jnp.arange(depth_rows)).astype(jnp.float32)
    factor = 4.0 / math.sqrt(NZ)
    return (factor / (1.0 + depth / NZ) ** 2, factor / (1.0 + depth / NZ) ** 3)


def coupling_forward(rim, magnetic_f, kernel, shape):
    depth_rows, x_rows, y_rows = shape
    pre_scale = stencil_sum(rim, kernel[0], depth_rows, x_rows, y_rows, False)
    pre_shift = stencil_sum(rim, kernel[1], depth_rows, x_rows, y_rows, False)
    scale = jnp.tanh(pre_scale)
    growth = jnp.exp(scale)
    return (scale, growth, magnetic_f * growth + pre_shift)


def local(whitened, observed, lower_x, lower_y, lower_z, coupling_kernel):
    factor_x, factor_y = (
        lax.all_gather(lower_x, "gx", axis=0, tiled=True),
        lax.all_gather(lower_y, "gx", axis=0, tiled=True),
    )

    def apply_depth(values):
        return jnp.einsum(
            "zk,fkxy->fzxy", lower_z, values, preferred_element_type=jnp.float32
        ).astype(jnp.bfloat16)

    def apply_across(values):
        return jnp.einsum(
            "xk,fzky->fzxy", factor_x, values, preferred_element_type=jnp.float32
        ).astype(jnp.bfloat16)

    def depth_adjoint(values):
        return jnp.einsum(
            "kz,fkxy->fzxy", lower_z, values, preferred_element_type=jnp.float32
        ).astype(jnp.bfloat16)

    def across_adjoint(values):
        return jnp.einsum(
            "kx,fzky->fzxy", factor_x, values, preferred_element_type=jnp.float32
        ).astype(jnp.bfloat16)

    start = whitened.astype(jnp.bfloat16)
    first = jnp.einsum("fzxk,yk->fzxy", start, factor_y, preferred_element_type=jnp.float32).astype(
        jnp.bfloat16
    )
    model = across_lines(depth_lines(first, apply_depth), apply_across)
    density = model[0]
    magnetic_f = model[1].astype(jnp.float32)
    depth_rows, x_rows, y_rows = density.shape
    rim = padded_2(density, (("gx", 1), ("gz", 0)), 1)
    rim = jnp.pad(rim, ((0, 0), (0, 0), (1, 1))).astype(jnp.float32)
    scale, growth, coupled = coupling_forward(
        rim, magnetic_f, coupling_kernel, (depth_rows, x_rows, y_rows)
    )
    weight_g, weight_m = depth_weights(lax.axis_index("gz") * depth_rows, depth_rows)
    part_g = jnp.einsum("z,zxy->xy", weight_g, density.astype(jnp.float32))
    part_m = jnp.einsum("z,zxy->xy", weight_m, coupled)
    predicted = lax.psum(jnp.stack([part_g, part_m]), "gz")
    misfit = predicted - observed
    back_g = weight_g[:, None, None] * misfit[0][None]
    back_m = weight_m[:, None, None] * misfit[1][None]
    back_scale = (back_m * magnetic_f * growth * (1.0 - scale * scale)).astype(jnp.bfloat16)
    back_shift = back_m.astype(jnp.bfloat16)
    cotangents = jnp.stack([back_scale, back_shift])
    outer = padded_2(cotangents, (("gx", 2), ("gz", 1)), 1)
    outer = jnp.pad(outer, ((0, 0), (0, 0), (0, 0), (1, 1))).astype(jnp.float32)
    spread_back = stencil_sum(outer[0], coupling_kernel[0], depth_rows, x_rows, y_rows, True)
    spread_back = spread_back + stencil_sum(
        outer[1], coupling_kernel[1], depth_rows, x_rows, y_rows, True
    )
    adjoint = jnp.stack([back_g + spread_back, back_m * growth]).astype(jnp.bfloat16)
    fourth = depth_lines(across_lines(adjoint, across_adjoint), depth_adjoint)
    gradient = whitened + jnp.einsum(
        "fzxk,ky->fzxy", fourth, factor_y, preferred_element_type=jnp.float32
    )
    return (gradient, misfit)


def solution(mesh):
    in_specs = (
        P(None, "gz", "gx", None),
        P(None, "gx", None),
        P("gx", None),
        P("gx", None),
        P(),
        P(),
    )
    out_specs = (P(None, "gz", "gx", None), P(None, "gx", None))
    return jax.shard_map(local, mesh=mesh, in_specs=in_specs, out_specs=out_specs, check_vma=False)
```

profile of v0, /device:TPU:0, one launch (start us, length us, event | category | flops | bytes accessed | tf_op | source)
XLA Modules:
  0.0 1367.9 jit_solution(581240853023325873)
XLA Ops:
  7.2 33.2 %all_gather.6 = bf16[512,512]{1,0:T(8,128)(2,1)S(1)} all-gather(bf16[64,512]{1,0:T(8,128)(2,1)} %param.9), channel_id=1, replica_groups=mesh['gx'=8,'gz'=4] {'gx'}, dimensions={0}, use_global_device_ids=true | all-gather | bytes 589824 | tf_op jit(solution)/shard_map/all_gather | solution.py:72
  41.2 7.8 fusion.77
  49.0 7.9 copy.51
  56.9 53.9 %all_to_all.141 = bf16[2,16,128,512]{2,1,0,3:T(8,128)(2,1)} all-to-all(bf16[2,16,128,512]{2,1,0,3:T(8,128)(2,1)} %copy.51), channel_id=1, replica_groups=mesh['gx'=8,'gz'=4] {'gz'}, dimensions={3} | all-to-all | bytes 8388608 | tf_op jit(solution)/shard_map/all_to_all | solution.py:24
  110.7 9.0 copy.52
  119.7 3.4 convert_bitcast_fusion.3
  123.1 2.7 copy.53
  125.8 51.6 %all_to_all.142 = bf16[2,64,128,128]{3,2,0,1:T(8,128)(2,1)} all-to-all(bf16[2,64,128,128]{3,2,0,1:T(8,128)(2,1)S(1)} %copy.53), channel_id=1, replica_groups=mesh['gx'=8,'gz'=4] {'gz'}, dimensions={1} | all-to-all | bytes 8388608 | tf_op jit(solution)/shard_map/all_to_all | solution.py:25
  177.4 7.8 copy.95
  185.3 5.7 all-to-all-start.2
  191.7 117.5 %all-to-all-done.2 = bf16[2,16,128,512]{2,1,0,3:T(8,128)(2,1)} async-done(((bf16[2,16,128,512]{2,1,0,3:T(8,128)(2,1)}), bf16[2,16,128,512]{2,1,0,3:T(8,128)(2,1)}, u32[]{:S(2)}, u32[]{:S(2)}) %all-to-all-start.2) | async-done | bytes 4194336 | tf_op jit(solution)/shard_map/all_to_all | solution.py:29
  309.2 6.9 copy.58
  316.1 7.3 all_to_all.113
  323.4 9.5 convert_bitcast_fusion.2
  332.8 12.9 copy.59
  345.7 10.5 reshape.38
  356.2 4.7 all-to-all-start.3
  363.3 90.1 %all-to-all-done.3 = bf16[8,2,131072]{2,1,0:T(2,128)(2,1)} async-done(((bf16[8,2,131072]{2,1,0:T(2,128)(2,1)}), bf16[8,2,131072]{2,1,0:T(2,128)(2,1)}, u32[]{:S(2)}, u32[]{:S(2)}) %all-to-all-start.3) | async-done | bytes 4194336 | tf_op jit(solution)/shard_map/all_to_all | solution.py:30
  453.4 10.3 reshape.39
  463.7 9.3 copy.97
  473.0 4.8 fusion.95
  478.4 2.8 fusion.96
  481.2 2.0 copy.63
  483.2 2.0 copy.64
  486.4 4.5 collective-permute-start
  491.7 3.0 copy.89
  494.7 1.8 copy.65
  496.5 1.8 copy.66
  503.2 2.8 copy.62
  506.6 11.2 fusion.10
  517.8 122.0 %add_add_fusion = (bf16[16,128,512]{1,2,0:T(8,128)(2,1)S(1)}, f32[16,128,512]{1,2,0:T(8,128)}) fusion(f32[16,128,512]{1,2,0:T(8,128)} %bitcast.166, f32[18,130,514]{1,2,0:T(8,128)} %fusion.10, f32[]{:T(128)} %bitcast.79, f32[]{:T(128)} %bitcast.78, f32[]{:T(128)} %bitcast.77, f32[]{:T(128)} %bitcast.76, f32[]{:T(128)} %bitcast.75, f32[]{:T(128)} %bitcast.74, ...), kind=kLoop, calls=%fused_computation.148 | loop fusion | flops 114294784 | bytes 123732184 | tf_op jit(solution)/shard_map/add | solution.py:66
  639.8 3.0 copy.91
  642.8 2.0 fusion.90
  645.7 35.0 %all-reduce.4.cloned.1.call-done = f32[2,128,512]{2,1,0:T(8,128)} async-done(((f32[2,128,512]{2,1,0:T(8,128)}), f32[2,128,512]{2,1,0:T(8,128)}) %all-reduce.4.cloned.1.call-update) | async-done | bytes 524304 | tf_op jit(solution)/shard_map/psum | solution.py:111
  683.3 6.4 fusion.81
  689.7 4.5 slice_maximum_fusion
  694.2 3.6 copy.70
  697.9 3.4 collective-permute-start.4
  701.3 4.0 copy.71
  706.6 3.2 copy.72
  711.1 3.2 copy.73
  714.3 2.9 pad_maximum_fusion.5
  720.2 3.2 collective-permute-done.7
  723.4 22.6 %fusion.1 = f32[2,18,130,514]{2,3,1,0:T(8,128)S(1)} fusion(bf16[2,1,130,512]{2,3,1,0:T(8,128)(2,1)} %collective-permute-done.7, bf16[2,1,130,512]{2,3,1,0:T(8,128)(2,1)S(1)} %collective-permute-done.6, bf16[2,16,1,512]{2,3,1,0:T(8,128)(2,1)} %copy.73, bf16[2,16,1,512]{2,3,1,0:T(8,128)(2,1)} %copy.72, bf16[1,16,128,512]{2,3,1,0:T(8,128)(2,1)S(1)} %multiply_convert_fusion, ...), kind=kLoop, calls=%fused_computation.8 | loop fusion | flops 50515920 | bytes 14414400 | tf_op jit(solution)/shard_map/convert_element_type | solution.py:119
  746.0 6.9 slice_bitcast_fusion.1
  752.9 196.9 %fusion.84 = bf16[1,16,128,512]{2,3,1,0:T(8,128)(2,1)S(1)} fusion(f32[18,130,514]{1,2,0:T(8,128)} %get-tuple-element.5, f32[]{:T(128)} %bitcast.79, f32[]{:T(128)} %bitcast.78, f32[]{:T(128)} %bitcast.77, f32[]{:T(128)} %bitcast.76, f32[]{:T(128)} %bitcast.75, f32[]{:T(128)} %bitcast.74, f32[]{:T(128)} %bitcast.73, f32[]{:T(128)} %bitcast.72, f32[]{:T(128)} %bitcast.71, ...), kind=kLoop, calls=%fused_computation.161 | loop fusion | flops 115343360 | bytes 228852000 | tf_op jit(solution)/shard_map/stack | solution.py:124
  950.2 2.7 copy.74
  952.9 97.5 %all_to_all.143 = bf16[2,16,128,512]{2,1,0,3:T(8,128)(2,1)S(1)} all-to-all(bf16[2,16,128,512]{2,1,0,3:T(8,128)(2,1)S(1)} %copy.74), channel_id=1, replica_groups=mesh['gx'=8,'gz'=4] {'gx'}, dimensions={3} | all-to-all | bytes 8388608 | tf_op jit(solution)/shard_map/all_to_all | solution.py:29
  1050.4 4.7 copy.76
  1055.1 7.4 all_to_all.120
  1062.6 8.4 convert_bitcast_fusion.1
  1071.0 12.9 copy.77
  1083.9 10.5 reshape.40
  1094.3 97.9 %all_to_all.144 = bf16[8,2,131072]{2,1,0:T(2,128)(2,1)} all-to-all(bf16[8,2,131072]{2,1,0:T(2,128)(2,1)} %reshape.40), channel_id=1, replica_groups=mesh['gx'=8,'gz'=4] {'gx'}, dimensions={0} | all-to-all | bytes 8388608 | tf_op jit(solution)/shard_map/all_to_all | solution.py:30
  1192.2 10.3 reshape.41
  1202.5 14.8 %copy.101 = bf16[2,16,128,8,64]{2,1,0,4,3:T(8,128)(2,1)} copy(bf16[2,16,128,8,64]{4,1,0,2,3:T(8,128)(2,1)} %bitcast.171) | data formatting | bytes 8388608 | tf_op jit(solution)/shard_map/all_to_all | solution.py:30
  1217.2 54.1 %all_to_all.145 = bf16[2,16,128,512]{2,1,0,3:T(8,128)(2,1)} all-to-all(bf16[2,16,128,512]{2,1,0,3:T(8,128)(2,1)} %bitcast.173), channel_id=1, replica_groups=mesh['gx'=8,'gz'=4] {'gz'}, dimensions={3} | all-to-all | bytes 8388608 | tf_op jit(solution)/shard_map/all_to_all | solution.py:24
  1271.3 9.0 copy.82
  1280.3 3.5 convert_bitcast_fusion
  1283.8 2.7 copy.84
  1286.5 50.7 %all_to_all.146 = bf16[2,64,128,128]{3,2,0,1:T(8,128)(2,1)S(1)} all-to-all(bf16[2,64,128,128]{3,2,0,1:T(8,128)(2,1)S(1)} %copy.84), channel_id=1, replica_groups=mesh['gx'=8,'gz'=4] {'gz'}, dimensions={1} | all-to-all | bytes 8388608 | tf_op jit(solution)/shard_map/all_to_all | solution.py:25
  1337.2 5.9 copy.109
  1343.2 7.2 all_to_all.132
  1350.4 10.4 convolution_add_fusion
  (63 shorter events, 21.2 us)
Async XLA Ops:
  7.2 112.5 %copy-start = (bf16[64,64]{1,0:T(8,128)(2,1)S(1)}, bf16[64,64]{1,0:T(8,128)(2,1)}, u32[]{:S(2)}) copy-start(bf16[64,64]{1,0:T(8,128)(2,1)} %param.10) | copy-start | bytes 24580
  40.4 0.8 copy-start.7
  185.3 123.9 %all-to-all-start.2 = ((bf16[2,16,128,512]{2,1,0,3:T(8,128)(2,1)}), bf16[2,16,128,512]{2,1,0,3:T(8,128)(2,1)}, u32[]{:S(2)}, u32[]{:S(2)}) async-start(bf16[2,16,128,512]{2,1,0,3:T(8,128)(2,1)} %bitcast.174), calls=%async_computation.2 | async-start | bytes 8388608 | tf_op jit(solution)/shard_map/all_to_all | solution.py:29
  191.0 132.4 %all-gather.2.cloned.1.call-start = ((), (), s32[]{:S(2)}) async-start(), calls=%async_computation.8 | async-start | bytes 2359296 | tf_op jit(solution)/shard_map/all_gather | solution.py:71
  356.2 4.9 copy-start.11
  356.2 97.2 %all-to-all-start.3 = ((bf16[8,2,131072]{2,1,0:T(2,128)(2,1)}), bf16[8,2,131072]{2,1,0:T(2,128)(2,1)}, u32[]{:S(2)}, u32[]{:S(2)}) async-start(bf16[8,2,131072]{2,1,0:T(2,128)(2,1)} %reshape.38), calls=%async_computation.3 | async-start | bytes 8388608 | tf_op jit(solution)/shard_map/all_to_all | solution.py:30
  360.9 319.8 %all-reduce.4.cloned.1.call-start = ((), (), s32[]{:S(2)}) async-start(), calls=%async_computation.9 | async-start | bytes 1048576 | tf_op jit(solution)/shard_map/psum | solution.py:111
  485.1 11.4 collective-permute-start.1
  486.4 8.3 collective-permute-start
  498.3 4.3 copy-start.5
  498.3 4.8 copy-start.4
  499.9 6.0 collective-permute-start.2
  501.4 4.6 collective-permute-start.3
  503.1 2.8 copy-start.2
  503.2 3.4 copy-start.3
  639.8 41.0 %copy-start.10 = (f32[2,128,512]{2,1,0:T(8,128)S(1)}, f32[2,128,512]{2,1,0:T(8,128)}, u32[]{:S(2)}) copy-start(f32[2,128,512]{2,1,0:T(8,128)} %param.7) | copy-start | bytes 1572868
  681.9 0.8 copy-start.9
  689.7 4.5 copy-start.1
  697.9 8.7 collective-permute-start.4
  705.3 5.8 collective-permute-start.5
  717.2 3.0 collective-permute-start.6
  718.5 4.9 collective-permute-start.7
  752.9 196.9 %copy-start.6 = (bf16[1,16,128,512]{2,3,1,0:T(8,128)(2,1)S(1)}, bf16[1,16,128,512]{2,3,1,0:T(8,128)(2,1)}, u32[]{:S(2)}) copy-start(bf16[1,16,128,512]{2,3,1,0:T(8,128)(2,1)} %get-tuple-element.11) | copy-start | bytes 6291460
  1055.1 7.4 copy-start.12
  1343.1 7.3 copy-start.8
Sparse Core Ops, SparseCore 0:
  193.9 102.6 all-gather.1
  645.8 34.8 all-reduce.3
where the time goes:
time: 1380 us; the launch traced here: 1370 us
  blocking collectives  439 us (32%)
  other arithmetic  376 us (27%)
  waiting for transfers between devices  248 us (18%)
  local copies, waits for them, and re-layouts  219 us (16%)
  matrix products  45.4 us (3%)
  starting transfers between devices  26.9 us (2%)
  between operations  14.6 us (1%)
    another operation x2, other arithmetic, local(): jnp.stack([back_g + spread_back, back_m * growth]).astype(jnp.bfloat16)  197 us
    add x1, other arithmetic, coupling_forward(): return (scale, growth, magnetic_f * growth + pre_shift)  122 us
    all_to_all x1, waiting for transfers between devices, across_lines(): lax.all_to_all(values, 'gx', split_axis=3, concat_axis=2, tiled=True)  117 us
    all_to_all x2, blocking collectives, depth_lines(): lax.all_to_all(values, 'gz', split_axis=3, concat_axis=1, tiled=True)  108 us
    all_to_all x2, blocking collectives, depth_lines(): lax.all_to_all(local_step(turned), 'gz', split_axis=1, concat_axis=3, til...  102 us
    all_to_all x1, blocking collectives, across_lines(): lax.all_to_all(local_step(turned), 'gx', split_axis=2, concat_axis=3, til...  97.9 us
    all_to_all x1, blocking collectives, across_lines(): lax.all_to_all(values, 'gx', split_axis=3, concat_axis=2, tiled=True)  97.5 us
    all_to_all x1, waiting for transfers between devices, across_lines(): lax.all_to_all(local_step(turned), 'gx', split_axis=2, concat_axis=3, til...  90.1 us
  transfers between devices with their start and end apart: 12, of which 6 were waited for; matrix products, arithmetic and copies ran while one was open for 2% of the time, Pallas kernels for 0%

commit v1 on v0

--- a/solution.py
+++ b/solution.py
@@ -1,3 +1,4 @@
+import functools
 import math
 import jax
 import jax.numpy as jnp
@@ -5,6 +6,27 @@
 from jax.sharding import PartitionSpec as P
 
 NZ = 64
+
+
+def meshes_follow(my_data, a_name):
+    current_block = lax.axis_size(a_name)
+    high = lax.axis_index(a_name)
+    block_last, spare = (current_block, high)
+    carry_in = my_data.shape[3] // block_last
+    u_next = list(my_data.shape)
+    u_next[3] = carry_in
+    m_next = u_next[2]
+    u_next[2] = m_next * block_last
+    newest = jnp.zeros(u_next, my_data.dtype)
+    for j0 in [*range(block_last)]:
+        h_now = lax.dynamic_slice_in_dim(my_data, (spare ^ j0) * carry_in, carry_in, axis=3)
+        if j0:
+            h_now = lax.ppermute(h_now, a_name, [(b, b ^ j0) for b in range(block_last)])
+        newest = lax.dynamic_update_slice_in_dim(newest, h_now, (spare ^ j0) * m_next, axis=2)
+    return newest
+
+
+edit_table_over_axis = functools.partial(meshes_follow, a_name="gx")
 
 
 def padded_2(x, sides, width):
@@ -26,7 +48,7 @@
 
 
 def across_lines(values, local_step):
-    turned = lax.all_to_all(values, "gx", split_axis=3, concat_axis=2, tiled=True)
+    turned = edit_table_over_axis(values)
     return lax.all_to_all(local_step(turned), "gx", split_axis=2, concat_axis=3, tiled=True)
 
 

time: 1380 us -> 1320 us (0.957)
  blocking collectives: 439 us -> 313 us
  waiting for transfers between devices: 248 us -> 294 us
  starting transfers between devices: 26.9 us -> 68.4 us
    ppermute x0 -> x14, waiting for transfers between devices: none -> 117 us  [meshes_follow(): lax.ppermute(h_now, a_name, [(b, b ^ j0) for b in range(block_last)])]
    all_to_all x1 -> x0, blocking collectives: 97.5 us -> none  [across_lines(): lax.all_to_all(values, 'gx', split_axis=3, concat_axis=2, tiled=True)]
    all_to_all x1, waiting for transfers between devices: 117 us -> 47.4 us  [depth_lines(): lax.all_to_all(local_step(turned), 'gz', split_axis=1, concat_axis=3, til...]
    all_to_all x2 -> x1, blocking collectives: 102 us -> 50.9 us  [depth_lines(): lax.all_to_all(local_step(turned), 'gz', split_axis=1, concat_axis=3, til...]
    all_to_all x4 -> x0, local copies, waits for them, and re-layouts: 26.3 us -> none  [across_lines(): lax.all_to_all(values, 'gx', split_axis=3, concat_axis=2, tiled=True)]
    ppermute x0 -> x14, starting transfers between devices: none -> 24.9 us  [meshes_follow(): lax.ppermute(h_now, a_name, [(b, b ^ j0) for b in range(block_last)])]
    all_to_all x1, blocking collectives: 97.9 us -> 121 us  [across_lines(): lax.all_to_all(local_step(turned), 'gx', split_axis=2, concat_axis=3, til...]
    all_to_all x1, starting transfers between devices: 4.68 us -> 22.4 us  [across_lines(): lax.all_to_all(local_step(turned), 'gx', split_axis=2, concat_axis=3, til...]
  transfers between devices with their start and end apart: 12 -> 26, of which waited for: 6 -> 16; matrix products, arithmetic and copies ran while one was open for 2% -> 3% of each run, Pallas kernels for 0% -> 0%
where the time goes in v1:
time: 1320 us; the launch traced here: 1310 us
  other arithmetic  372 us (28%)
  blocking collectives  313 us (24%)
  waiting for transfers between devices  294 us (22%)
  local copies, waits for them, and re-layouts  206 us (16%)
  starting transfers between devices  68.4 us (5%)
  matrix products  43.1 us (3%)
  between operations  14.8 us (1%)
    another operation x3, other arithmetic, local(): jnp.stack([back_g + spread_back, back_m * growth]).astype(jnp.bfloat16)  197 us
    all_to_all x1, blocking collectives, across_lines(): lax.all_to_all(local_step(turned), 'gx', split_axis=2, concat_axis=3, til...  121 us
    add x1, other arithmetic, coupling_forward(): return (scale, growth, magnetic_f * growth + pre_shift)  119 us
    ppermute x14, waiting for transfers between devices, meshes_follow(): lax.ppermute(h_now, a_name, [(b, b ^ j0) for b in range(block_last)])  117 us
    all_to_all x2, blocking collectives, depth_lines(): lax.all_to_all(values, 'gz', split_axis=3, concat_axis=1, tiled=True)  108 us
    all_to_all x1, waiting for transfers between devices, across_lines(): lax.all_to_all(local_step(turned), 'gx', split_axis=2, concat_axis=3, til...  89.8 us
    all_to_all x1, blocking collectives, depth_lines(): lax.all_to_all(local_step(turned), 'gz', split_axis=1, concat_axis=3, til...  50.9 us
    unnamed x35, local copies, waits for them, and re-layouts  48.6 us
  transfers between devices with their start and end apart: 26, of which 16 were waited for; matrix products, arithmetic and copies ran while one was open for 3% of the time, Pallas kernels for 0%

profile of v1, /device:TPU:0, one launch (start us, length us, event | category | flops | bytes accessed | tf_op | source)
XLA Modules:
  0.0 1311.3 jit_solution(2802043343012531742)
XLA Ops:
  7.2 33.2 %all_gather.6 = bf16[512,512]{1,0:T(8,128)(2,1)S(1)} all-gather(bf16[64,512]{1,0:T(8,128)(2,1)} %param.9), channel_id=1, replica_groups=mesh['gx'=8,'gz'=4] {'gx'}, dimensions={0}, use_global_device_ids=true | all-gather | bytes 589824 | tf_op jit(solution)/shard_map/all_gather | solution.py:94
  41.2 7.8 fusion.77
  49.0 7.9 copy.75
  56.8 53.8 %all_to_all.105 = bf16[2,16,128,512]{2,1,0,3:T(8,128)(2,1)} all-to-all(bf16[2,16,128,512]{2,1,0,3:T(8,128)(2,1)} %copy.75), channel_id=1, replica_groups=mesh['gx'=8,'gz'=4] {'gz'}, dimensions={3} | all-to-all | bytes 8388608 | tf_op jit(solution)/shard_map/all_to_all | solution.py:46
  110.7 9.0 copy.76
  119.7 3.4 convert_bitcast_fusion.3
  123.1 4.7 copy.77
  127.8 4.9 all-to-all-start.1
  133.5 47.4 %all-to-all-done.1 = bf16[2,64,128,128]{3,2,0,1:T(8,128)(2,1)} async-done(((bf16[2,64,128,128]{3,2,0,1:T(8,128)(2,1)}), bf16[2,64,128,128]{3,2,0,1:T(8,128)(2,1)}, u32[]{:S(2)}, u32[]{:S(2)}) %all-to-all-start.1) | async-done | bytes 4194336 | tf_op jit(solution)/shard_map/all_to_all | solution.py:47
  181.0 6.2 copy.78
  201.3 6.1 collective-permute-done
  207.4 3.2 collective-permute-start.5
  211.4 20.2 %collective-permute-done.1 = bf16[2,16,128,64]{2,3,1,0:T(8,128)(2,1)S(1)} collective-permute-done((bf16[2,16,128,64]{2,3,1,0:T(8,128)(2,1)}, bf16[2,16,128,64]{2,3,1,0:T(8,128)(2,1)S(1)}, u32[]{:S(2)}, u32[]{:S(2)}) %collective-permute-start.1) | collective-permute-done | bytes 524320 | tf_op jit(solution)/shard_map/ppermute | solution.py:24
  232.4 7.8 collective-permute-done.2
  241.9 28.6 %collective-permute-done.4 = bf16[2,16,128,64]{2,3,1,0:T(8,128)(2,1)S(1)} collective-permute-done((bf16[2,16,128,64]{2,3,1,0:T(8,128)(2,1)}, bf16[2,16,128,64]{2,3,1,0:T(8,128)(2,1)S(1)}, u32[]{:S(2)}, u32[]{:S(2)}) %collective-permute-start.4) | collective-permute-done | bytes 524320 | tf_op jit(solution)/shard_map/ppermute | solution.py:24
  273.0 9.4 convert_bitcast_fusion.2
  282.4 12.9 copy.79
  295.3 10.6 reshape.38
  305.9 22.4 %all-to-all-start.2 = ((bf16[8,2,131072]{2,1,0:T(2,128)(2,1)}), bf16[8,2,131072]{2,1,0:T(2,128)(2,1)}, u32[]{:S(2)}, u32[]{:S(2)}) async-start(bf16[8,2,131072]{2,1,0:T(2,128)(2,1)} %reshape.38), calls=%async_computation.2 | async-start | bytes 8388608 | tf_op jit(solution)/shard_map/all_to_all | solution.py:52
  331.0 89.8 %all-to-all-done.2 = bf16[8,2,131072]{2,1,0:T(2,128)(2,1)} async-done(((bf16[8,2,131072]{2,1,0:T(2,128)(2,1)}), bf16[8,2,131072]{2,1,0:T(2,128)(2,1)}, u32[]{:S(2)}, u32[]{:S(2)}) %all-to-all-start.2) | async-done | bytes 4194336 | tf_op jit(solution)/shard_map/all_to_all | solution.py:52
  420.7 10.3 reshape.39
  431.0 9.3 copy.111
  440.3 4.8 fusion.104
  445.7 2.8 fusion.105
  456.7 3.0 copy.106
  466.4 3.0 collective-permute-start.9
  469.9 2.8 copy.82
  473.3 11.1 fusion.10
  484.4 118.6 %add_add_fusion = (bf16[16,128,512]{1,2,0:T(8,128)(2,1)S(1)}, f32[16,128,512]{1,2,0:T(8,128)}) fusion(f32[16,128,512]{1,2,0:T(8,128)} %bitcast.151, f32[18,130,514]{1,2,0:T(8,128)} %fusion.10, f32[]{:T(128)} %bitcast.74, f32[]{:T(128)} %bitcast.73, f32[]{:T(128)} %bitcast.72, f32[]{:T(128)} %bitcast.71, f32[]{:T(128)} %bitcast.70, f32[]{:T(128)} %bitcast.69, ...), kind=kLoop, calls=%fused_computation.163 | loop fusion | flops 114294784 | bytes 123732184 | tf_op jit(solution)/shard_map/add | solution.py:88
  603.0 3.0 copy.108
  608.9 35.3 %all-reduce.4.cloned.1.call-done = f32[2,128,512]{2,1,0:T(8,128)} async-done(((f32[2,128,512]{2,1,0:T(8,128)}), f32[2,128,512]{2,1,0:T(8,128)}) %all-reduce.4.cloned.1.call-update) | async-done | bytes 524304 | tf_op jit(solution)/shard_map/psum | solution.py:133
  646.8 6.4 fusion.81
  653.2 4.5 slice_maximum_fusion
  657.7 3.6 copy.90
  661.3 3.4 collective-permute-start.11
  664.7 3.9 copy.91
  669.9 3.3 copy.92
  674.4 3.2 copy.93
  677.6 2.9 pad_maximum_fusion.4
  683.5 3.2 collective-permute-done.14
  686.7 22.6 %fusion.1 = f32[2,18,130,514]{2,3,1,0:T(8,128)S(1)} fusion(bf16[2,1,130,512]{2,3,1,0:T(8,128)(2,1)} %collective-permute-done.14, bf16[2,1,130,512]{2,3,1,0:T(8,128)(2,1)S(1)} %collective-permute-done.13, bf16[2,16,1,512]{2,3,1,0:T(8,128)(2,1)} %copy.93, bf16[2,16,1,512]{2,3,1,0:T(8,128)(2,1)} %copy.92, bf16[1,16,128,512]{2,3,1,0:T(8,128)(2,1)S(1)} %multiply_convert_fusion, ...), kind=kLoop, calls=%fused_computation.8 | loop fusion | flops 50515920 | bytes 14414400 | tf_op jit(solution)/shard_map/convert_element_type | solution.py:141
  709.3 6.9 slice_bitcast_fusion.1
  716.2 196.3 %fusion.84 = bf16[1,16,128,512]{2,3,1,0:T(8,128)(2,1)S(1)} fusion(f32[18,130,514]{1,2,0:T(8,128)} %get-tuple-element.5, f32[]{:T(128)} %bitcast.74, f32[]{:T(128)} %bitcast.73, f32[]{:T(128)} %bitcast.72, f32[]{:T(128)} %bitcast.71, f32[]{:T(128)} %bitcast.70, f32[]{:T(128)} %bitcast.69, f32[]{:T(128)} %bitcast.68, f32[]{:T(128)} %bitcast.67, f32[]{:T(128)} %bitcast.66, ...), kind=kLoop, calls=%fused_computation.176 | loop fusion | flops 115343360 | bytes 228852000 | tf_op jit(solution)/shard_map/stack | solution.py:146
  914.8 2.4 collective-permute-start.15
  918.9 2.9 collective-permute-start.18
  924.4 3.8 collective-permute-start.20
  928.4 19.1 %collective-permute-done.16 = bf16[2,16,128,64]{2,3,1,0:T(8,128)(2,1)S(1)} collective-permute-done((bf16[2,16,128,64]{2,3,1,0:T(8,128)(2,1)S(1)}, bf16[2,16,128,64]{2,3,1,0:T(8,128)(2,1)S(1)}, u32[]{:S(2)}, u32[]{:S(2)}) %collective-permute-start.16) | collective-permute-done | bytes 524320 | tf_op jit(solution)/shard_map/ppermute | solution.py:24
  949.6 7.2 collective-permute-done.17
  959.0 14.0 %collective-permute-done.20 = bf16[2,16,128,64]{2,3,1,0:T(8,128)(2,1)S(1)} collective-permute-done((bf16[2,16,128,64]{2,3,1,0:T(8,128)(2,1)S(1)}, bf16[2,16,128,64]{2,3,1,0:T(8,128)(2,1)S(1)}, u32[]{:S(2)}, u32[]{:S(2)}) %collective-permute-start.20) | collective-permute-done | bytes 524320 | tf_op jit(solution)/shard_map/ppermute | solution.py:24
  973.1 11.0 collective-permute-done.21
  984.3 6.1 convert_bitcast_fusion.1
  990.5 13.3 %copy.94 = bf16[2,16,1024,64]{3,1,0,2:T(8,128)(2,1)} copy(bf16[2,16,1024,64]{2,3,1,0:T(8,128)(2,1)} %convert_bitcast_fusion.1) | data formatting | bytes 8388608 | tf_op jit(solution)/shard_map/convert_element_type | solution.py:115
  1003.8 10.5 reshape.40
  1014.3 121.4 %all_to_all.106 = bf16[8,2,131072]{2,1,0:T(2,128)(2,1)} all-to-all(bf16[8,2,131072]{2,1,0:T(2,128)(2,1)} %reshape.40), channel_id=1, replica_groups=mesh['gx'=8,'gz'=4] {'gx'}, dimensions={0} | all-to-all | bytes 8388608 | tf_op jit(solution)/shard_map/all_to_all | solution.py:52
  1135.7 10.3 reshape.41
  1146.0 14.8 %copy.114 = bf16[2,16,128,8,64]{2,1,0,4,3:T(8,128)(2,1)} copy(bf16[2,16,128,8,64]{4,1,0,2,3:T(8,128)(2,1)} %bitcast.156) | data formatting | bytes 8388608 | tf_op jit(solution)/shard_map/all_to_all | solution.py:52
  1160.8 53.8 %all_to_all.107 = bf16[2,16,128,512]{2,1,0,3:T(8,128)(2,1)} all-to-all(bf16[2,16,128,512]{2,1,0,3:T(8,128)(2,1)} %bitcast.158), channel_id=1, replica_groups=mesh['gx'=8,'gz'=4] {'gz'}, dimensions={3} | all-to-all | bytes 8388608 | tf_op jit(solution)/shard_map/all_to_all | solution.py:46
  1214.6 9.0 copy.99
  1223.6 3.5 convert_bitcast_fusion
  1227.1 2.7 copy.101
  1229.8 50.9 %all_to_all.108 = bf16[2,64,128,128]{3,2,0,1:T(8,128)(2,1)S(1)} all-to-all(bf16[2,64,128,128]{3,2,0,1:T(8,128)(2,1)S(1)} %copy.101), channel_id=1, replica_groups=mesh['gx'=8,'gz'=4] {'gz'}, dimensions={1} | all-to-all | bytes 8388608 | tf_op jit(solution)/shard_map/all_to_all | solution.py:47
  1280.7 5.9 copy.122
  1286.6 7.3 all_to_all.98
  1293.9 10.4 convolution_add_fusion
  (106 shorter events, 62.8 us)
Async XLA Ops:
  7.2 112.5 %copy-start = (bf16[64,64]{1,0:T(8,128)(2,1)S(1)}, bf16[64,64]{1,0:T(8,128)(2,1)}, u32[]{:S(2)}) copy-start(bf16[64,64]{1,0:T(8,128)(2,1)} %param.10) | copy-start | bytes 24580
  40.4 0.8 copy-start.8
  127.8 53.1 %all-to-all-start.1 = ((bf16[2,64,128,128]{3,2,0,1:T(8,128)(2,1)}), bf16[2,64,128,128]{3,2,0,1:T(8,128)(2,1)}, u32[]{:S(2)}, u32[]{:S(2)}) async-start(bf16[2,64,128,128]{3,2,0,1:T(8,128)(2,1)} %copy.77), calls=%async_computation.1 | async-start | bytes 8388608 | tf_op jit(solution)/shard_map/all_to_all | solution.py:47
  132.7 140.3 %all-gather.2.cloned.1.call-start = ((), (), s32[]{:S(2)}) async-start(), calls=%async_computation.6 | async-start | bytes 2359296 | tf_op jit(solution)/shard_map/all_gather | solution.py:93
  187.1 2.2 copy-start.6
  191.7 2.0 copy-start.10
  193.7 13.7 %collective-permute-start = (bf16[2,16,128,64]{2,3,1,0:T(8,128)(2,1)}, bf16[2,16,128,64]{2,3,1,0:T(8,128)(2,1)S(1)}, u32[]{:S(2)}, u32[]{:S(2)}) collective-permute-start(bf16[2,16,128,64]{2,3,1,0:T(8,128)(2,1)} %get-tuple-element.30), channel_id=1, source_target_pairs={{0,4},{4,0},{8,12},{12,8},{16,20},{20,16},{24,28},{28,24},{1,5},{5... | collective-permute-start | bytes 1572872 | tf_op jit(solution)/shard_map/ppermute | solution.py:24
  195.4 36.2 %collective-permute-start.1 = (bf16[2,16,128,64]{2,3,1,0:T(8,128)(2,1)}, bf16[2,16,128,64]{2,3,1,0:T(8,128)(2,1)S(1)}, u32[]{:S(2)}, u32[]{:S(2)}) collective-permute-start(bf16[2,16,128,64]{2,3,1,0:T(8,128)(2,1)} %get-tuple-element.29), channel_id=1, source_target_pairs={{0,8},{4,12},{8,0},{12,4},{16,24},{20,28},{24,16},{28,20},{1,9},{5... | collective-permute-start | bytes 1572872 | tf_op jit(solution)/shard_map/ppermute | solution.py:24
  195.4 44.8 %collective-permute-start.2 = (bf16[2,16,128,64]{2,3,1,0:T(8,128)(2,1)}, bf16[2,16,128,64]{2,3,1,0:T(8,128)(2,1)S(1)}, u32[]{:S(2)}, u32[]{:S(2)}) collective-permute-start(bf16[2,16,128,64]{2,3,1,0:T(8,128)(2,1)} %get-tuple-element.28), channel_id=1, source_target_pairs={{0,12},{4,8},{8,4},{12,0},{16,28},{20,24},{24,20},{28,16},{1,13},{... | collective-permute-start | bytes 1572872 | tf_op jit(solution)/shard_map/ppermute | solution.py:24
  197.2 43.8 %collective-permute-start.3 = (bf16[2,16,128,64]{2,3,1,0:T(8,128)(2,1)}, bf16[2,16,128,64]{2,3,1,0:T(8,128)(2,1)S(1)}, u32[]{:S(2)}, u32[]{:S(2)}) collective-permute-start(bf16[2,16,128,64]{2,3,1,0:T(8,128)(2,1)} %get-tuple-element.27), channel_id=1, source_target_pairs={{0,16},{4,20},{8,24},{12,28},{16,0},{20,4},{24,8},{28,12},{1,17},{... | collective-permute-start | bytes 1572872 | tf_op jit(solution)/shard_map/ppermute | solution.py:24
  199.2 71.2 %collective-permute-start.4 = (bf16[2,16,128,64]{2,3,1,0:T(8,128)(2,1)}, bf16[2,16,128,64]{2,3,1,0:T(8,128)(2,1)S(1)}, u32[]{:S(2)}, u32[]{:S(2)}) collective-permute-start(bf16[2,16,128,64]{2,3,1,0:T(8,128)(2,1)} %get-tuple-element.26), channel_id=1, source_target_pairs={{0,20},{4,16},{8,28},{12,24},{16,4},{20,0},{24,12},{28,8},{1,21},{... | collective-permute-start | bytes 1572872 | tf_op jit(solution)/shard_map/ppermute | solution.py:24
  207.4 63.9 %collective-permute-start.5 = (bf16[2,16,128,64]{2,3,1,0:T(8,128)(2,1)}, bf16[2,16,128,64]{2,3,1,0:T(8,128)(2,1)S(1)}, u32[]{:S(2)}, u32[]{:S(2)}) collective-permute-start(bf16[2,16,128,64]{2,3,1,0:T(8,128)(2,1)} %get-tuple-element.25), channel_id=1, source_target_pairs={{0,24},{4,28},{8,16},{12,20},{16,8},{20,12},{24,0},{28,4},{1,25},{... | collective-permute-start | bytes 1572872 | tf_op jit(solution)/shard_map/ppermute | solution.py:24
  231.6 40.6 %collective-permute-start.6 = (bf16[2,16,128,64]{2,3,1,0:T(8,128)(2,1)S(1)}, bf16[2,16,128,64]{2,3,1,0:T(8,128)(2,1)S(1)}, u32[]{:S(2)}, u32[]{:S(2)}) collective-permute-start(bf16[2,16,128,64]{2,3,1,0:T(8,128)(2,1)S(1)} %get-tuple-element.24), channel_id=1, source_target_pairs={{0,28},{4,24},{8,20},{12,16},{16,12},{20,8},{24,4},{28,0},{1,29},{... | collective-permute-start | bytes 1572872 | tf_op jit(solution)/shard_map/ppermute | solution.py:24
  305.9 23.0 %copy-start.13 = (f32[2,3,3,3]{3,0,2,1:T(2,128)S(1)}, f32[2,3,3,3]{3,0,2,1:T(2,128)}, u32[]{:S(2)}) copy-start(f32[2,3,3,3]{3,0,2,1:T(2,128)} %param.11) | copy-start | bytes 652
  305.9 114.8 %all-to-all-start.2 = ((bf16[8,2,131072]{2,1,0:T(2,128)(2,1)}), bf16[8,2,131072]{2,1,0:T(2,128)(2,1)}, u32[]{:S(2)}, u32[]{:S(2)}) async-start(bf16[8,2,131072]{2,1,0:T(2,128)(2,1)} %reshape.38), calls=%async_computation.2 | async-start | bytes 8388608 | tf_op jit(solution)/shard_map/all_to_all | solution.py:52
  328.3 316.0 %all-reduce.4.cloned.1.call-start = ((), (), s32[]{:S(2)}) async-start(), calls=%async_computation.7 | async-start | bytes 1048576 | tf_op jit(solution)/shard_map/psum | solution.py:133
  450.5 9.2 collective-permute-start.7
  454.7 6.8 collective-permute-start.8
  463.4 6.1 copy-start.7
  463.4 6.5 copy-start.5
  464.9 7.7 collective-permute-start.10
  466.4 6.3 collective-permute-start.9
  469.9 2.8 copy-start.3
  469.9 3.4 copy-start.4
  603.0 41.2 %copy-start.12 = (f32[2,128,512]{2,1,0:T(8,128)S(1)}, f32[2,128,512]{2,1,0:T(8,128)}, u32[]{:S(2)}) copy-start(f32[2,128,512]{2,1,0:T(8,128)} %param.7) | copy-start | bytes 1572868
  645.3 0.8 copy-start.11
  653.2 4.5 copy-start.1
  661.3 8.6 collective-permute-start.11
  668.6 5.8 collective-permute-start.12
  680.5 3.0 collective-permute-start.13
  681.8 4.9 collective-permute-start.14
  912.5 1.6 copy-start.2
  914.8 9.6 collective-permute-start.15
  917.2 30.3 %collective-permute-start.16 = (bf16[2,16,128,64]{2,3,1,0:T(8,128)(2,1)S(1)}, bf16[2,16,128,64]{2,3,1,0:T(8,128)(2,1)S(1)}, u32[]{:S(2)}, u32[]{:S(2)}) collective-permute-start(bf16[2,16,128,64]{2,3,1,0:T(8,128)(2,1)S(1)} %get-tuple-element.15), channel_id=1, source_target_pairs={{0,8},{4,12},{8,0},{12,4},{16,24},{20,28},{24,16},{28,20},{1,9},{5... | collective-permute-start | bytes 1572872 | tf_op jit(solution)/shard_map/ppermute | solution.py:24
  918.7 38.0 %collective-permute-start.17 = (bf16[2,16,128,64]{2,3,1,0:T(8,128)(2,1)S(1)}, bf16[2,16,128,64]{2,3,1,0:T(8,128)(2,1)S(1)}, u32[]{:S(2)}, u32[]{:S(2)}) collective-permute-start(bf16[2,16,128,64]{2,3,1,0:T(8,128)(2,1)S(1)} %get-tuple-element.16), channel_id=1, source_target_pairs={{0,12},{4,8},{8,4},{12,0},{16,28},{20,24},{24,20},{28,16},{1,13},{... | collective-permute-start | bytes 1572872 | tf_op jit(solution)/shard_map/ppermute | solution.py:24
  918.9 65.4 %copy-start.14 = (bf16[1024,1024]{1,0:T(8,128)(2,1)S(1)}, bf16[1024,1024]{1,0:T(8,128)(2,1)}, u32[]{:S(2)}) copy-start(bf16[1024,1024]{1,0:T(8,128)(2,1)} %all-gather.2.cloned.1.call-done) | copy-start | bytes 6291460
  918.9 38.0 %collective-permute-start.18 = (bf16[2,16,128,64]{2,3,1,0:T(8,128)(2,1)S(1)}, bf16[2,16,128,64]{2,3,1,0:T(8,128)(2,1)S(1)}, u32[]{:S(2)}, u32[]{:S(2)}) collective-permute-start(bf16[2,16,128,64]{2,3,1,0:T(8,128)(2,1)S(1)} %get-tuple-element.18), channel_id=1, source_target_pairs={{0,16},{4,20},{8,24},{12,28},{16,0},{20,4},{24,8},{28,12},{1,17},{... | collective-permute-start | bytes 1572872 | tf_op jit(solution)/shard_map/ppermute | solution.py:24
  921.9 37.0 %collective-permute-start.19 = (bf16[2,16,128,64]{2,3,1,0:T(8,128)(2,1)S(1)}, bf16[2,16,128,64]{2,3,1,0:T(8,128)(2,1)S(1)}, u32[]{:S(2)}, u32[]{:S(2)}) collective-permute-start(bf16[2,16,128,64]{2,3,1,0:T(8,128)(2,1)S(1)} %get-tuple-element.19), channel_id=1, source_target_pairs={{0,20},{4,16},{8,28},{12,24},{16,4},{20,0},{24,12},{28,8},{1,21},{... | collective-permute-start | bytes 1572872 | tf_op jit(solution)/shard_map/ppermute | solution.py:24
  924.4 48.6 %collective-permute-start.20 = (bf16[2,16,128,64]{2,3,1,0:T(8,128)(2,1)S(1)}, bf16[2,16,128,64]{2,3,1,0:T(8,128)(2,1)S(1)}, u32[]{:S(2)}, u32[]{:S(2)}) collective-permute-start(bf16[2,16,128,64]{2,3,1,0:T(8,128)(2,1)S(1)} %get-tuple-element.17), channel_id=1, source_target_pairs={{0,24},{4,28},{8,16},{12,20},{16,8},{20,12},{24,0},{28,4},{1,25},{... | collective-permute-start | bytes 1572872 | tf_op jit(solution)/shard_map/ppermute | solution.py:24
  947.5 36.6 %collective-permute-start.21 = (bf16[2,16,128,64]{2,3,1,0:T(8,128)(2,1)S(1)}, bf16[2,16,128,64]{2,3,1,0:T(8,128)(2,1)S(1)}, u32[]{:S(2)}, u32[]{:S(2)}) collective-permute-start(bf16[2,16,128,64]{2,3,1,0:T(8,128)(2,1)S(1)} %get-tuple-element.12), channel_id=1, source_target_pairs={{0,28},{4,24},{8,20},{12,16},{16,12},{20,8},{24,4},{28,0},{1,29},{... | collective-permute-start | bytes 1572872 | tf_op jit(solution)/shard_map/ppermute | solution.py:24
  1286.6 7.3 copy-start.9
Sparse Core Ops, SparseCore 0:
  135.7 50.8 all-gather.1
  609.0 35.1 all-reduce.3
